TPU v7x, 32 devices: a whole 2x2x4 slice. The times are simulated.
32 devices in a mesh: section: 2 (over core), expert: 4 (over y, x), replica: 4 (over z).
Axes of the slice: x: 2, y: 2, z: 4, core: 2. Of those that a mesh axis runs over, the one named last changes fastest.
Arguments:
- forward_tokens: bfloat16 [2, 2048, 2048], P('section', ('expert', 'replica')), may hold values from -6 to 6
- forward_routes: int32 [2, 2048, 1], P('section', ('expert', 'replica')), may hold values from 0 to 3; in each aligned block of 128 rows (0 to 127, 128 to 255, ..., all dimensions but the last counted through in order) at most 48 rows name the same one
- forward_gates: float32 [2, 2048, 1], P('section', ('expert', 'replica')), may hold values from 0.1 to 1
- backward_cotangent: bfloat16 [2, 2048, 2048], P('section', ('expert', 'replica')), may hold values from -6 to 6
- backward_routes: int32 [2, 2048, 1], P('section', ('expert', 'replica')), may hold values from 0 to 3; in each aligned block of 128 rows (0 to 127, 128 to 255, ..., all dimensions but the last counted through in order) at most 48 rows name the same one
- backward_gates: float32 [2, 2048, 1], P('section', ('expert', 'replica')), may hold values from 0.1 to 1
- saved_rows: bfloat16 [2, 4, 768, 2048], P('section', 'expert', 'replica'), may hold values from -6 to 6
- gate_weight: bfloat16 [2, 4, 2048, 384], P('section', 'expert'), may hold values from -0.125 to 0.125
- up_weight: bfloat16 [2, 4, 2048, 384], P('section', 'expert'), may hold values from -0.125 to 0.125
- down_weight: bfloat16 [2, 4, 2048, 384], P('section', 'expert'), may hold values from -0.3125 to 0.3125
Outputs:
- forward_out: bfloat16 [2, 2048, 2048], P('section', ('expert', 'replica'))
- received_grad: bfloat16 [2, 2048, 2048], P('section', ('expert', 'replica'))
- expert_grads: bfloat16 [2, 4, 2048, 768], P('section', 'expert', 'replica')
Inputs may be any that keep to these rules, and one draw needn't show every extreme that they name: `forward_routes`: each is an expert in flight. Among the rows of one device, no expert is named more than 48 times, and some expert reaches 48. `backward_routes`: each is an expert in flight. Among the rows of one device, no expert is named more than 48 times, and some expert reaches 48.
All inputs are finite; a program needn't handle non-finite values.
Results may differ from a plain program's by a relative error of at most 0.017.
Values may be sent and summed in bfloat16 or wider, within the bound.
A program may use at most 64 MiB of HBM per device.

v0:
```python
import jax
import jax.numpy as jnp
from jax import lax
from jax.sharding import PartitionSpec as P


def from_behind(value, axis, steps):
    count = lax.axis_size(axis)
    pairs = [(source, (source + steps) % count) for source in range(count)]
    return lax.ppermute(value, axis, pairs)


def route_table(routes, experts, capacity):
    flat_ids = routes.reshape(-1)
    member = (flat_ids[:, None] == jnp.arange(experts, dtype=jnp.int32)[None, :]).astype(jnp.int32)
    earlier = jnp.cumsum(member, axis=0) - member
    slot_index = jnp.sum(earlier * member, axis=1)
    target = flat_ids * capacity + slot_index
    return (target[:, None] == jnp.arange(experts * capacity, dtype=jnp.int32)[None, :]).astype(
        jnp.bfloat16
    )


def pack_rows(table, values):
    packed = lax.dot_general(
        table, values, (((0,), (0,)), ((), ())), preferred_element_type=jnp.float32
    )
    return packed.astype(jnp.bfloat16)


def expert_forward(row_block, w_gate, w_up, w_down):
    gate_pre = jnp.dot(row_block, w_gate, preferred_element_type=jnp.float32)
    up_pre = jnp.dot(row_block, w_up, preferred_element_type=jnp.float32)
    hidden = (gate_pre * jax.nn.sigmoid(gate_pre) * up_pre).astype(jnp.bfloat16)
    result = lax.dot_general(
        hidden, w_down, (((1,), (1,)), ((), ())), preferred_element_type=jnp.float32
    )
    return result.astype(jnp.bfloat16)


def expert_backward(row_block, cot_block, w_gate, w_up, w_down):
    gate_pre = jnp.dot(row_block, w_gate, preferred_element_type=jnp.float32)
    up_pre = jnp.dot(row_block, w_up, preferred_element_type=jnp.float32)
    sigma = jax.nn.sigmoid(gate_pre)
    hidden_grad = jnp.dot(cot_block, w_down, preferred_element_type=jnp.float32)
    up_grad = (hidden_grad * gate_pre * sigma).astype(jnp.bfloat16)
    gate_grad = (hidden_grad * up_pre * sigma * (1.0 + gate_pre * (1.0 - sigma))).astype(
        jnp.bfloat16
    )
    contract = (((1,), (1,)), ((), ()))
    row_grad = lax.dot_general(gate_grad, w_gate, contract, preferred_element_type=jnp.float32)
    row_grad = row_grad + lax.dot_general(
        up_grad, w_up, contract, preferred_element_type=jnp.float32
    )
    return (row_grad.astype(jnp.bfloat16), gate_grad, up_grad)


def shards(
    forward_tokens,
    forward_routes,
    forward_gates,
    backward_cotangent,
    backward_routes,
    backward_gates,
    saved_rows,
    gate_weight,
    up_weight,
    down_weight,
):
    experts = lax.axis_size("expert")
    saved = saved_rows[0, 0]
    capacity = saved.shape[0] // experts
    width = saved.shape[1]
    fanout = forward_routes.shape[2]
    w_gate = gate_weight[0, 0]
    w_up = up_weight[0, 0]
    w_down = down_weight[0, 0]
    tokens_here = forward_tokens[0]
    count_here = tokens_here.shape[0]
    forward_table = route_table(forward_routes[0], experts, capacity)
    copies = jnp.repeat(tokens_here, fanout, axis=0)
    forward_buffer = pack_rows(forward_table, copies).reshape(experts, capacity, width)
    cotangent_here = backward_cotangent[0]
    backward_table = route_table(backward_routes[0], experts, capacity)
    scaled = backward_gates[0] * jnp.repeat(cotangent_here.astype(jnp.float32), fanout, axis=0)
    backward_buffer = pack_rows(backward_table, scaled.astype(jnp.bfloat16)).reshape(
        experts, capacity, width
    )
    arrived_fwd = lax.all_to_all(forward_buffer, "expert", split_axis=0, concat_axis=0, tiled=True)
    arrived_bwd = lax.all_to_all(backward_buffer, "expert", split_axis=0, concat_axis=0, tiled=True)
    fwd_rows = arrived_fwd.reshape(experts * capacity, width)
    cot_rows = arrived_bwd.reshape(experts * capacity, width)
    outputs = expert_forward(fwd_rows, w_gate, w_up, w_down).reshape(experts, capacity, width)
    row_grad, gate_grad, up_grad = expert_backward(saved, cot_rows, w_gate, w_up, w_down)
    row_grad = row_grad.reshape(experts, capacity, width)
    back_fwd = lax.all_to_all(outputs, "expert", split_axis=0, concat_axis=0, tiled=True)
    back_bwd = lax.all_to_all(row_grad, "expert", split_axis=0, concat_axis=0, tiled=True)
    returned = jnp.dot(
        forward_table, back_fwd.reshape(-1, width), preferred_element_type=jnp.float32
    )
    weighted = returned * forward_gates[0]
    mixed = jnp.sum(weighted.reshape(count_here, fanout, width), axis=1)
    forward_out = (tokens_here.astype(jnp.float32) + mixed).astype(jnp.bfloat16)
    gathered = jnp.dot(
        backward_table, back_bwd.reshape(-1, width), preferred_element_type=jnp.float32
    )
    summed = jnp.sum(gathered.reshape(count_here, fanout, width), axis=1)
    local_grad = (cotangent_here.astype(jnp.float32) + summed).astype(jnp.bfloat16)
    received = from_behind(local_grad, "section", -1)
    both_grads = jnp.concatenate([gate_grad, up_grad], axis=1)
    weight_grads = lax.psum_scatter(
        lax.dot_general(
            saved, both_grads, (((0,), (0,)), ((), ())), preferred_element_type=jnp.float32
        ).astype(jnp.bfloat16),
        "replica",
        scatter_dimension=0,
        tiled=True,
    )
    return (forward_out[None], received[None], weight_grads[None, None])


def solution(mesh):
    in_specs = (
        P("section", ("expert", "replica"), None),
        P("section", ("expert", "replica"), None),
        P("section", ("expert", "replica"), None),
        P("section", ("expert", "replica"), None),
        P("section", ("expert", "replica"), None),
        P("section", ("expert", "replica"), None),
        P("section", "expert", "replica", None),
        P("section", "expert", None, None),
        P("section", "expert", None, None),
        P("section", "expert", None, None),
    )
    out_specs = (
        P("section", ("expert", "replica"), None),
        P("section", ("expert", "replica"), None),
        P("section", "expert", "replica", None),
    )
    return jax.shard_map(shards, mesh=mesh, in_specs=in_specs, out_specs=out_specs, check_vma=False)
```

profile of v0, /device:TPU:0, one launch (start us, length us, event | category | flops | bytes accessed | tf_op | source)
XLA Modules:
  0.0 106.4 jit_solution(9522595846635523115)
XLA Ops:
  7.2 0.0 copy-start
  7.2 0.0 copy-start.1
  7.2 0.9 fusion.59
  8.1 0.2 reduce_window_sum.18
  8.3 0.8 select_reduce_fusion
  9.1 0.7 multiply_add_fusion
  9.8 2.4 %convolution_convert_fusion.1 = bf16[192,2048]{1,0:T(8,128)(2,1)} fusion(bf16[1,128,2048]{2,1,0:T(8,128)(2,1)} %param.13, f32[128]{0:T(128)} %bitcast.93, s32[128]{0:T(128)S(1)} %multiply_add_fusion), kind=kOutput, calls=%fused_computation.4 | convolution fusion | flops 101867520 | bytes 1311744 | tf_op jit(solution)/shard_map/dot_general | solution.py:25
  12.2 5.2 %all-to-all-start.2 = ((bf16[4,48,2048]{2,1,0:T(8,128)(2,1)}), bf16[4,48,2048]{2,1,0:T(8,128)(2,1)}, u32[]{:S(2)}, u32[]{:S(2)}) async-start(bf16[4,48,2048]{2,1,0:T(8,128)(2,1)} %bitcast.85), calls=%async_computation.2 | async-start | bytes 1572864 | tf_op jit(solution)/shard_map/all_to_all | solution.py:90
  17.3 0.0 reduce-scatter.2.cloned.1.call-start
  17.3 0.0 copy-done.1
  17.3 2.4 %fusion.16 = f32[192,384]{1,0:T(8,128)} fusion(bf16[1,1,2048,384]{3,2,1,0:T(8,128)(2,1)S(1)} %copy-done.1, bf16[1,1,192,2048]{3,2,1,0:T(8,128)(2,1)} %param.16), kind=kOutput, calls=%fused_computation.23 | convolution fusion | flops 301989888 | bytes 2654208 | tf_op jit(solution)/shard_map/dot_general | solution.py:42
  19.8 9.0 %all-to-all-done.2 = bf16[4,48,2048]{2,1,0:T(8,128)(2,1)} async-done(((bf16[4,48,2048]{2,1,0:T(8,128)(2,1)}), bf16[4,48,2048]{2,1,0:T(8,128)(2,1)}, u32[]{:S(2)}, u32[]{:S(2)}) %all-to-all-start.2) | async-done | bytes 786464 | tf_op jit(solution)/shard_map/all_to_all | solution.py:90
  28.8 0.0 copy-start.2
  28.8 0.0 copy-start.4
  28.8 2.3 %multiply_convert_fusion = (bf16[192,384]{1,0:T(8,128)(2,1)S(1)}, f32[192,384]{1,0:T(8,128)S(1)}) fusion(f32[192,384]{1,0:T(8,128)} %fusion.16, bf16[192,2048]{1,0:T(8,128)(2,1)} %bitcast.16, bf16[1,1,2048,384]{3,2,1,0:T(8,128)(2,1)} %param.19), kind=kOutput, calls=%fused_computation.44 | convolution fusion | flops 302432256 | bytes 3096576 | tf_op jit(solution)/shard_map/dot_general | solution.py:45
  31.1 0.0 copy-done
  31.1 0.0 copy-done.2
  31.1 0.0 copy-done.4
  31.1 0.6 fusion.35
  31.7 2.7 %fusion = bf16[2048,768]{0,1:T(8,128)(2,1)} fusion(bf16[1,1,192,2048]{3,2,1,0:T(8,128)(2,1)S(1)} %copy-done.2, bf16[192,384]{1,0:T(8,128)(2,1)S(1)} %get-tuple-element.6, bf16[192,384]{1,0:T(8,128)(2,1)S(1)} %fusion.35), kind=kOutput, calls=%fused_computation.1 | convolution fusion | flops 606142464 | bytes 4227072 | tf_op jit(solution)/shard_map/dot_general | solution.py:112
  34.4 0.0 copy-start.5
  34.4 0.0 reduce-scatter.2.cloned.1.call-update
  34.5 0.6 copy-done.5
  35.1 0.7 fusion.62
  35.8 1.0 reduce_window_sum.17
  36.8 0.2 select_reduce_fusion.1
  37.0 2.4 %convolution_convert_fusion.2 = bf16[192,2048]{1,0:T(8,128)(2,1)} fusion(bf16[1,128,2048]{2,1,0:T(8,128)(2,1)} %param.10, s32[128]{0:T(128)S(1)} %multiply_add_fusion.1), kind=kOutput, calls=%fused_computation.5 | convolution fusion | flops 101081088 | bytes 1311232 | tf_op jit(solution)/shard_map/dot_general | solution.py:25
  39.4 4.2 %all-to-all-start = ((bf16[4,48,2048]{2,1,0:T(8,128)(2,1)}), bf16[4,48,2048]{2,1,0:T(8,128)(2,1)}, u32[]{:S(2)}, u32[]{:S(2)}) async-start(bf16[4,48,2048]{2,1,0:T(8,128)(2,1)} %bitcast.84), calls=%async_computation | async-start | bytes 1572864 | tf_op jit(solution)/shard_map/all_to_all | solution.py:89
  43.6 0.7 fusion.14
  44.3 1.6 %fusion.1 = bf16[192,2048]{1,0:T(8,128)(2,1)} fusion(f32[192,2048]{1,0:T(8,128)S(1)} %fusion.14, bf16[192,384]{1,0:T(8,128)(2,1)S(1)} %get-tuple-element.6, bf16[1,1,2048,384]{3,2,1,0:T(8,128)(2,1)S(1)} %copy-done), kind=kOutput, calls=%fused_computation.3 | convolution fusion | flops 302776320 | bytes 4079616 | tf_op jit(solution)/shard_map/dot_general | solution.py:52
  45.9 8.3 %all-to-all-done = bf16[4,48,2048]{2,1,0:T(8,128)(2,1)} async-done(((bf16[4,48,2048]{2,1,0:T(8,128)(2,1)}), bf16[4,48,2048]{2,1,0:T(8,128)(2,1)}, u32[]{:S(2)}, u32[]{:S(2)}) %all-to-all-start) | async-done | bytes 786464 | tf_op jit(solution)/shard_map/all_to_all | solution.py:89
  54.2 4.2 %all-to-all-start.3 = ((bf16[4,48,2048]{2,1,0:T(8,128)(2,1)}), bf16[4,48,2048]{2,1,0:T(8,128)(2,1)}, u32[]{:S(2)}, u32[]{:S(2)}) async-start(bf16[4,48,2048]{2,1,0:T(8,128)(2,1)} %bitcast.86), calls=%async_computation.3 | async-start | bytes 1572864 | tf_op jit(solution)/shard_map/all_to_all | solution.py:97
  58.4 1.7 %fusion.18 = f32[192,384]{1,0:T(8,128)S(1)} fusion(bf16[192,2048]{1,0:T(8,128)(2,1)} %bitcast.3, bf16[1,1,2048,384]{3,2,1,0:T(8,128)(2,1)S(1)} %copy-done.1), kind=kOutput, calls=%fused_computation.25 | convolution fusion | flops 301989888 | bytes 2654208 | tf_op jit(solution)/shard_map/dot_general | solution.py:32
  60.1 3.7 %convolution_convert_fusion.3 = bf16[192,2048]{1,0:T(8,128)(2,1)} fusion(bf16[1,1,2048,384]{3,2,1,0:T(8,128)(2,1)} %param.19, bf16[192,2048]{1,0:T(8,128)(2,1)} %bitcast.3, bf16[1,1,2048,384]{3,2,1,0:T(8,128)(2,1)S(1)} %copy-done, f32[192,384]{1,0:T(8,128)S(1)} %fusion.18), kind=kOutput, calls=%fused_computation.6 | convolution fusion | flops 604815360 | bytes 5013504 | tf_op jit(solution)/shard_map/dot_general | solution.py:35
  63.9 4.9 %all-to-all-done.3 = bf16[4,48,2048]{2,1,0:T(8,128)(2,1)} async-done(((bf16[4,48,2048]{2,1,0:T(8,128)(2,1)}), bf16[4,48,2048]{2,1,0:T(8,128)(2,1)}, u32[]{:S(2)}, u32[]{:S(2)}) %all-to-all-start.3) | async-done | bytes 786464 | tf_op jit(solution)/shard_map/all_to_all | solution.py:97
  68.8 0.0 copy-start.3
  68.8 0.0 copy-start.6
  68.8 3.6 %all-to-all-start.1 = ((bf16[4,48,2048]{2,1,0:T(8,128)(2,1)}), bf16[4,48,2048]{2,1,0:T(8,128)(2,1)S(1)}, u32[]{:S(2)}, u32[]{:S(2)}) async-start(bf16[4,48,2048]{2,1,0:T(8,128)(2,1)} %bitcast.88), calls=%async_computation.1 | async-start | bytes 1572864 | tf_op jit(solution)/shard_map/all_to_all | solution.py:96
  72.4 2.4 %fusion.5 = bf16[128,2048]{1,0:T(8,128)(2,1)} fusion(bf16[192,2048]{1,0:T(8,128)(2,1)} %bitcast.19, bf16[1,128,2048]{2,1,0:T(8,128)(2,1)} %param.13, s32[128]{0:T(128)S(1)} %multiply_add_fusion), kind=kOutput, calls=%fused_computation.12 | convolution fusion | flops 101474304 | bytes 1835520 | tf_op jit(solution)/shard_map/dot_general | solution.py:104
  74.8 0.0 collective-permute-start
  74.9 7.8 %all-to-all-done.1 = bf16[4,48,2048]{2,1,0:T(8,128)(2,1)S(1)} async-done(((bf16[4,48,2048]{2,1,0:T(8,128)(2,1)}), bf16[4,48,2048]{2,1,0:T(8,128)(2,1)S(1)}, u32[]{:S(2)}, u32[]{:S(2)}) %all-to-all-start.1) | async-done | bytes 786464 | tf_op jit(solution)/shard_map/all_to_all | solution.py:96
  82.6 0.0 copy-done.3
  82.7 0.0 copy-done.6
  82.7 1.2 %fusion.4 = bf16[1,128,2048]{2,1,0:T(8,128)(2,1)} fusion(bf16[192,2048]{1,0:T(8,128)(2,1)S(1)} %bitcast.83, bf16[1,128,2048]{2,1,0:T(8,128)(2,1)S(1)} %copy-done.3, f32[128]{0:T(128)S(1)} %bitcast.94, s32[128]{0:T(128)S(1)} %multiply_add_fusion.1), kind=kOutput, calls=%fused_computation.11 | convolution fusion | flops 101736448 | bytes 1836032 | tf_op jit(solution)/shard_map/dot_general | solution.py:98
  83.8 0.0 collective-permute-done
  83.8 11.6 %reduce-scatter.2.cloned.1.call-done = bf16[512,768]{0,1:T(8,128)(2,1)} async-done(((bf16[2048,768]{0,1:T(8,128)(2,1)}), bf16[512,768]{0,1:T(8,128)(2,1)}) %reduce-scatter.2.cloned.1.call-update) | async-done | bytes 786448 | tf_op jit(solution)/shard_map/reduce_scatter | solution.py:111
  95.4 2.3 %copy.13 = bf16[1,1,512,768]{3,2,1,0:T(8,128)(2,1)} copy(bf16[1,1,512,768]{2,3,1,0:T(8,128)(2,1)} %bitcast.87) | data formatting | bytes 1572864
  97.7 1.9 %copy.15 = bf16[1,128,2048]{2,1,0:T(8,128)(2,1)} copy(bf16[1,128,2048]{2,1,0:T(8,128)(2,1)} %bitcast.20) | data formatting | bytes 1048576
  (1 shorter events, 0.0 us)
Async XLA Ops:
  7.2 23.9 %copy-start = (bf16[1,1,2048,384]{3,2,1,0:T(8,128)(2,1)S(1)}, bf16[1,1,2048,384]{3,2,1,0:T(8,128)(2,1)}, u32[]{:S(2)}) copy-start(bf16[1,1,2048,384]{3,2,1,0:T(8,128)(2,1)} %param.18) | copy-start | bytes 4718596
  7.2 10.2 %copy-start.1 = (bf16[1,1,2048,384]{3,2,1,0:T(8,128)(2,1)S(1)}, bf16[1,1,2048,384]{3,2,1,0:T(8,128)(2,1)}, u32[]{:S(2)}) copy-start(bf16[1,1,2048,384]{3,2,1,0:T(8,128)(2,1)} %param.17) | copy-start | bytes 4718596
  12.2 16.6 %all-to-all-start.2 = ((bf16[4,48,2048]{2,1,0:T(8,128)(2,1)}), bf16[4,48,2048]{2,1,0:T(8,128)(2,1)}, u32[]{:S(2)}, u32[]{:S(2)}) async-start(bf16[4,48,2048]{2,1,0:T(8,128)(2,1)} %bitcast.85), calls=%async_computation.2 | async-start | bytes 1572864 | tf_op jit(solution)/shard_map/all_to_all | solution.py:90
  17.3 78.0 %reduce-scatter.2.cloned.1.call-start = ((), (), s32[]{:S(2)}) async-start(), calls=%async_computation.5 | async-start | bytes 3932160 | tf_op jit(solution)/shard_map/reduce_scatter | solution.py:111
  28.8 2.4 %copy-start.2 = (bf16[1,1,192,2048]{3,2,1,0:T(8,128)(2,1)S(1)}, bf16[1,1,192,2048]{3,2,1,0:T(8,128)(2,1)}, u32[]{:S(2)}) copy-start(bf16[1,1,192,2048]{3,2,1,0:T(8,128)(2,1)} %param.16) | copy-start | bytes 2359300
  28.8 2.4 %copy-start.4 = (f32[192,384]{1,0:T(8,128)S(1)}, f32[192,384]{1,0:T(8,128)}, u32[]{:S(2)}) copy-start(f32[192,384]{1,0:T(8,128)} %fusion.16) | copy-start | bytes 884740
  34.4 0.7 copy-start.5
  39.4 14.8 %all-to-all-start = ((bf16[4,48,2048]{2,1,0:T(8,128)(2,1)}), bf16[4,48,2048]{2,1,0:T(8,128)(2,1)}, u32[]{:S(2)}, u32[]{:S(2)}) async-start(bf16[4,48,2048]{2,1,0:T(8,128)(2,1)} %bitcast.84), calls=%async_computation | async-start | bytes 1572864 | tf_op jit(solution)/shard_map/all_to_all | solution.py:89
  54.2 14.5 %all-to-all-start.3 = ((bf16[4,48,2048]{2,1,0:T(8,128)(2,1)}), bf16[4,48,2048]{2,1,0:T(8,128)(2,1)}, u32[]{:S(2)}, u32[]{:S(2)}) async-start(bf16[4,48,2048]{2,1,0:T(8,128)(2,1)} %bitcast.86), calls=%async_computation.3 | async-start | bytes 1572864 | tf_op jit(solution)/shard_map/all_to_all | solution.py:97
  68.8 13.9 %copy-start.3 = (bf16[1,128,2048]{2,1,0:T(8,128)(2,1)S(1)}, bf16[1,128,2048]{2,1,0:T(8,128)(2,1)}, u32[]{:S(2)}) copy-start(bf16[1,128,2048]{2,1,0:T(8,128)(2,1)} %param.10) | copy-start | bytes 1572868
  68.8 13.9 %copy-start.6 = (f32[1,128,1]{1,2,0:T(1,128)S(1)}, f32[1,128,1]{1,2,0:T(1,128)}, u32[]{:S(2)}) copy-start(f32[1,128,1]{1,2,0:T(1,128)} %param.12) | copy-start | bytes 1540
  68.8 13.9 %all-to-all-start.1 = ((bf16[4,48,2048]{2,1,0:T(8,128)(2,1)}), bf16[4,48,2048]{2,1,0:T(8,128)(2,1)S(1)}, u32[]{:S(2)}, u32[]{:S(2)}) async-start(bf16[4,48,2048]{2,1,0:T(8,128)(2,1)} %bitcast.88), calls=%async_computation.1 | async-start | bytes 1572864 | tf_op jit(solution)/shard_map/all_to_all | solution.py:96
  74.8 9.0 %collective-permute-start = (bf16[128,2048]{1,0:T(8,128)(2,1)}, bf16[128,2048]{1,0:T(8,128)(2,1)}, u32[]{:S(2)}, u32[]{:S(2)}) collective-permute-start(bf16[128,2048]{1,0:T(8,128)(2,1)} %fusion.5), channel_id=1, source_target_pairs={{0,16},{16,0},{1,17},{17,1},{2,18},{18,2},{3,19},{19,3},{4,20},{20... | collective-permute-start | bytes 1572872 | tf_op jit(solution)/shard_map/ppermute | solution.py:10
Sparse Core Ops, SparseCore 0:
  34.6 60.7 reduce-scatter.1
where the time goes:
time: 107 us; the launch traced here: 106 us
  waiting for transfers between devices  41.6 us (39%)
  matrix products  24.2 us (23%)
  starting transfers between devices  17.2 us (16%)
  between operations  14.1 us (13%)
  local copies, waits for them, and re-layouts  4.82 us (5%)
  other arithmetic  4.45 us (4%)
    reduce_scatter x1, waiting for transfers between devices, shards(): lax.psum_scatter(lax.dot_general(saved, both_grads, (((0,), (0,)), ((), (...  11.6 us
    all_to_all x1, waiting for transfers between devices, shards(): lax.all_to_all(backward_buffer, 'expert', split_axis=0, concat_axis=0, ti...  8.99 us
    all_to_all x1, waiting for transfers between devices, shards(): lax.all_to_all(forward_buffer, 'expert', split_axis=0, concat_axis=0, til...  8.31 us
    all_to_all x1, waiting for transfers between devices, shards(): lax.all_to_all(outputs, 'expert', split_axis=0, concat_axis=0, tiled=True)  7.8 us
    all_to_all x1, starting transfers between devices, shards(): lax.all_to_all(backward_buffer, 'expert', split_axis=0, concat_axis=0, ti...  5.16 us
    all_to_all x1, waiting for transfers between devices, shards(): lax.all_to_all(row_grad, 'expert', split_axis=0, concat_axis=0, tiled=True)  4.88 us
    unnamed x16, local copies, waits for them, and re-layouts  4.82 us
    dot_general x2, matrix products, pack_rows(): lax.dot_general(table, values, (((0,), (0,)), ((), ())), preferred_elemen...  4.82 us
  transfers between devices with their start and end apart: 6, of which 5 were waited for; matrix products, arithmetic and copies ran while one was open for 17% of the time, Pallas kernels for 0%

commit v1 on v0

v1 whole, which is shorter than its diff:
```python
import functools

import jax
import jax.numpy as jnp
from jax import lax
from jax.experimental import pallas as pl
from jax.experimental.pallas import tpu as pltpu
from jax.sharding import PartitionSpec as P

MESH = pl.DeviceIdType.MESH
BF16, F32 = jnp.bfloat16, jnp.float32


def flipped(index, mask):
    for bit in range(mask.bit_length()):
        if (mask >> bit) & 1:
            index = index + (1 << bit) * (1 - 2 * ((index // (1 << bit)) % 2))
    return index


def route_slots(routes, experts, cap):
    tokens = routes.shape[1]
    height = -(-experts // 16) * 16
    member = (lax.broadcasted_iota(jnp.int32, (height, tokens), 0) == routes).astype(F32)
    above = lax.broadcasted_iota(jnp.int32, (tokens, tokens), 0)
    across = lax.broadcasted_iota(jnp.int32, (tokens, tokens), 1)
    before = (above < across).astype(F32).astype(BF16)
    earlier = jnp.dot(member.astype(BF16), before, preferred_element_type=F32)
    slot = jnp.sum(earlier * member, axis=0, keepdims=True)
    row = routes.astype(F32) * cap + slot
    return row, to_column(row)


def to_column(row):
    tokens = row.shape[1]
    above = lax.broadcasted_iota(jnp.int32, (tokens, tokens), 0)
    across = lax.broadcasted_iota(jnp.int32, (tokens, tokens), 1)
    return jnp.sum(jnp.where(above == across, row, 0.0), axis=1, keepdims=True)


def spread_table(column, rows):
    across = lax.broadcasted_iota(jnp.int32, (column.shape[0], rows), 1).astype(F32)
    return (across == column).astype(F32).astype(BF16)


def transposed_dot(a, b):
    return lax.dot_general(a, b, (((1,), (1,)), ((), ())), preferred_element_type=F32)


def kernel(
    sections, experts, replicas, cap,
    f_routes, f_gates, b_routes, b_gates, tokens_hbm, cot_hbm, saved_hbm, gate_hbm, up_hbm, down_hbm,
    out_hbm, received_hbm, grads_hbm,
    tokens, cot, saved, w_gu, w_down, f_send, f_recv, b_send, b_recv,
    o_send, o_recv, r_send, r_recv, x_all, g_all, pre, out_v, local_v, grads_v,
    local_sem, a2a_send, a2a_recv, x_send, x_recv, g_send, g_recv, s_send, s_recv, out_sem,
):
    section, me, rep = lax.axis_index("section"), lax.axis_index("expert"), lax.axis_index("replica")
    count, width = tokens.shape
    rows = experts * cap
    hidden_units = w_down.shape[1]
    share = width // replicas
    chunk = min(512, width)

    barrier = pltpu.get_barrier_semaphore()
    greeted = 0
    for k in range(1, experts):
        pl.semaphore_signal(barrier, inc=1, device_id={"expert": flipped(me, k)}, device_id_type=MESH)
        greeted += 1
    for k in range(1, replicas):
        pl.semaphore_signal(barrier, inc=1, device_id={"replica": (rep + k) % replicas}, device_id_type=MESH)
        greeted += 1
    for k in sorted({1, sections - 1}):
        pl.semaphore_signal(barrier, inc=1, device_id={"section": (section + k) % sections}, device_id_type=MESH)
        greeted += 1

    loads = [
        pltpu.make_async_copy(src, dst, local_sem.at[i])
        for i, (src, dst) in enumerate([
            (cot_hbm, cot),
            (tokens_hbm, tokens),
            (saved_hbm, saved),
            (gate_hbm, w_gu.at[:, pl.ds(0, hidden_units)]),
            (up_hbm, w_gu.at[:, pl.ds(hidden_units, hidden_units)]),
            (down_hbm, w_down),
            (saved_hbm.at[:, pl.ds(pl.multiple_of(rep * share, share), share)],
             x_all.at[pl.ds(pl.multiple_of(rep * rows, rows), rows)]),
        ])
    ]
    for load in loads:
        load.start()

    def block(ref, index):
        return ref.at[pl.ds(pl.multiple_of(index * cap, cap), cap)]

    def exchange(phase, k, src, dst):
        other = flipped(me, k)
        return pltpu.make_async_remote_copy(
            src_ref=block(src, other), dst_ref=block(dst, me),
            send_sem=a2a_send.at[phase, k], recv_sem=a2a_recv.at[phase, k],
            device_id={"expert": other}, device_id_type=MESH,
        )

    order = list(range(experts - 1, 0, -1))

    def pack(row, values, index):
        down = lax.broadcasted_iota(jnp.int32, (cap, count), 0).astype(F32) + (index * cap).astype(F32)
        table = (down == row).astype(F32).astype(BF16)
        return jnp.dot(table, values, preferred_element_type=F32).astype(BF16)

    b_row, b_column = route_slots(b_routes[...], experts, cap)
    b_scale = to_column(b_gates[...])
    loads[0].wait()
    scaled = (b_scale * cot[...].astype(F32)).astype(BF16)
    phases = [[], [], [], []]
    for k in order:
        block(b_send, flipped(me, k))[...] = pack(b_row, scaled, flipped(me, k))
        if k == order[0]:
            pl.semaphore_wait(barrier, greeted)
        copy = exchange(0, k, b_send, b_recv)
        copy.start()
        phases[0].append(copy)
    x_copies = []
    for k in range(1, replicas):
        other = (rep + k) % replicas
        copy = pltpu.make_async_remote_copy(
            src_ref=saved_hbm.at[:, pl.ds(pl.multiple_of(other * share, share), share)],
            dst_ref=x_all.at[pl.ds(pl.multiple_of(rep * rows, rows), rows)],
            send_sem=x_send.at[k], recv_sem=x_recv.at[k],
            device_id={"replica": other}, device_id_type=MESH,
        )
        copy.start()
        x_copies.append(copy)
    block(b_recv, me)[...] = pack(b_row, scaled, me)

    f_row, f_column = route_slots(f_routes[...], experts, cap)
    f_scale = to_column(f_gates[...])
    loads[1].wait()
    for k in order:
        block(f_send, flipped(me, k))[...] = pack(f_row, tokens[...], flipped(me, k))
        copy = exchange(1, k, f_send, f_recv)
        copy.start()
        phases[1].append(copy)
    block(f_recv, me)[...] = pack(f_row, tokens[...], me)

    loads[2].wait()
    loads[3].wait()
    loads[4].wait()
    pre[...] = jnp.dot(saved[...], w_gu[...], preferred_element_type=F32)
    loads[5].wait()

    for copy in phases[0]:
        copy.wait_recv()
    hidden_grad = jnp.dot(b_recv[...], w_down[...], preferred_element_type=F32)
    gate_pre, up_pre = pre[:, :hidden_units], pre[:, hidden_units:]
    sigma = jax.nn.sigmoid(gate_pre)
    mine = pl.ds(pl.multiple_of(rep * rows, rows), rows)
    g_all[mine, hidden_units:] = (hidden_grad * gate_pre * sigma).astype(BF16)
    g_all[mine, :hidden_units] = (
        hidden_grad * up_pre * sigma * (1.0 + gate_pre * (1.0 - sigma))
    ).astype(BF16)

    def pass_on(source, side):
        where = pl.ds(pl.multiple_of(source * rows, rows), rows)
        other = rep + (1 if side == 0 else -1)
        return pltpu.make_async_remote_copy(
            src_ref=g_all.at[where], dst_ref=g_all.at[where],
            send_sem=g_send.at[side, source], recv_sem=g_recv.at[source],
            device_id={"replica": other}, device_id_type=MESH,
        )

    @pl.when(rep < replicas - 1)
    def _():
        pass_on(rep, 0).start()

    @pl.when(rep > 0)
    def _():
        pass_on(rep, 1).start()

    for c in range(0, width, chunk):
        r_send[:, c:c + chunk] = transposed_dot(g_all[mine, :], w_gu[c:c + chunk, :]).astype(BF16)
    for k in order:
        copy = exchange(2, k, r_send, r_recv)
        copy.start()
        phases[2].append(copy)
    block(r_recv, me)[...] = block(r_send, me)[...]

    for copy in phases[1]:
        copy.wait_recv()
    pre[...] = jnp.dot(f_recv[...], w_gu[...], preferred_element_type=F32)
    gate_pre, up_pre = pre[:, :hidden_units], pre[:, hidden_units:]
    hidden = (gate_pre * jax.nn.sigmoid(gate_pre) * up_pre).astype(BF16)
    for c in range(0, width, chunk):
        o_send[:, c:c + chunk] = transposed_dot(hidden, w_down[c:c + chunk, :]).astype(BF16)
    for k in order:
        copy = exchange(3, k, o_send, o_recv)
        copy.start()
        phases[3].append(copy)
    block(o_recv, me)[...] = block(o_send, me)[...]

    def relay(step):
        low, high = rep - step, rep + step

        @pl.when(low >= 0)
        def _():
            pass_on(low, 0).wait_recv()

            @pl.when(rep < replicas - 1)
            def _():
                pass_on(low, 0).start()

        @pl.when(high < replicas)
        def _():
            pass_on(high, 1).wait_recv()

            @pl.when(rep > 0)
            def _():
                pass_on(high, 1).start()

    relay(1)

    for copy in phases[2]:
        copy.wait_recv()
    back = jnp.dot(spread_table(b_column, rows), r_recv[...], preferred_element_type=F32)
    local_v[...] = (cot[...].astype(F32) + back).astype(BF16)
    onward = pltpu.make_async_remote_copy(
        src_ref=local_v, dst_ref=received_hbm, send_sem=s_send, recv_sem=s_recv,
        device_id={"section": (section + sections - 1) % sections}, device_id_type=MESH,
    )
    onward.start()

    for step in range(2, replicas):
        relay(step)
    for copy in x_copies:
        copy.wait_recv()
    loads[6].wait()
    grads_v[...] = lax.dot_general(
        x_all[...], g_all[...], (((0,), (0,)), ((), ())), preferred_element_type=F32
    ).astype(BF16)
    store_grads = pltpu.make_async_copy(grads_v, grads_hbm, out_sem.at[0])
    store_grads.start()

    for copy in phases[3]:
        copy.wait_recv()
    back = jnp.dot(spread_table(f_column, rows), o_recv[...], preferred_element_type=F32)
    out_v[...] = (tokens[...].astype(F32) + f_scale * back).astype(BF16)
    store_out = pltpu.make_async_copy(out_v, out_hbm, out_sem.at[1])
    store_out.start()

    for phase in phases:
        for copy in phase:
            copy.wait_send()
    for copy in x_copies:
        copy.wait_send()
    for source in range(replicas):
        @pl.when((rep >= source) & (rep < replicas - 1))
        def _():
            pass_on(source, 0).wait_send()

        @pl.when((rep <= source) & (rep > 0))
        def _():
            pass_on(source, 1).wait_send()
    onward.wait()
    store_grads.wait()
    store_out.wait()


def solution(mesh):
    sections, experts, replicas = mesh.shape["section"], mesh.shape["expert"], mesh.shape["replica"]

    def shards(
        forward_tokens, forward_routes, forward_gates, backward_cotangent, backward_routes, backward_gates,
        saved_rows, gate_weight, up_weight, down_weight,
    ):
        count, width = forward_tokens.shape[1:]
        hidden_units = gate_weight.shape[3]
        slots = saved_rows.shape[2] // experts
        cap = -(-slots // 16) * 16
        saved = saved_rows[0, 0]
        if cap != slots:
            saved = jnp.pad(saved.reshape(experts, slots, width), ((0, 0), (0, cap - slots), (0, 0)))
            saved = saved.reshape(experts * cap, width)
        rows = experts * cap
        share = width // replicas
        buffer = pltpu.VMEM((rows, width), BF16)
        dma = pltpu.SemaphoreType.DMA
        whole = pl.BlockSpec(memory_space=pltpu.VMEM)
        anywhere = pl.BlockSpec(memory_space=pl.ANY)
        out, received, grads = pl.pallas_call(
            functools.partial(kernel, sections, experts, replicas, cap),
            out_shape=[
                jax.ShapeDtypeStruct((count, width), BF16),
                jax.ShapeDtypeStruct((count, width), BF16),
                jax.ShapeDtypeStruct((share, 2 * hidden_units), BF16),
            ],
            in_specs=[whole] * 4 + [anywhere] * 6,
            out_specs=[anywhere] * 3,
            scratch_shapes=[
                pltpu.VMEM((count, width), BF16),
                pltpu.VMEM((count, width), BF16),
                buffer,
                pltpu.VMEM((width, 2 * hidden_units), BF16),
                pltpu.VMEM((width, hidden_units), BF16),
                buffer, buffer, buffer, buffer,
                buffer, buffer, buffer, buffer,
                pltpu.VMEM((replicas * rows, share), BF16),
                pltpu.VMEM((replicas * rows, 2 * hidden_units), BF16),
                pltpu.VMEM((rows, 2 * hidden_units), F32),
                pltpu.VMEM((count, width), BF16),
                pltpu.VMEM((count, width), BF16),
                pltpu.VMEM((share, 2 * hidden_units), BF16),
                dma((7,)),
                dma((4, experts)),
                dma((4, experts)),
                dma((replicas,)),
                dma((replicas,)),
                dma((2, replicas)),
                dma((replicas,)),
                dma,
                dma,
                dma((2,)),
            ],
            compiler_params=pltpu.CompilerParams(
                collective_id=0, has_side_effects=True, vmem_limit_bytes=48 * 1024 * 1024
            ),
        )(
            forward_routes.reshape(1, count), forward_gates.reshape(1, count),
            backward_routes.reshape(1, count), backward_gates.reshape(1, count),
            forward_tokens[0], backward_cotangent[0], saved,
            gate_weight[0, 0], up_weight[0, 0], down_weight[0, 0],
        )
        return out[None], received[None], grads[None, None]

    tokens = P("section", ("expert", "replica"), None)
    weights = P("section", "expert", None, None)
    rows = P("section", "expert", "replica", None)
    return jax.shard_map(
        shards, mesh=mesh, in_specs=(tokens,) * 6 + (rows,) + (weights,) * 3,
        out_specs=(tokens, tokens, rows), check_vma=False,
    )
```

time: 107 us -> 56.3 us (0.53)
  Pallas kernels: 0 us -> 45.7 us
  waiting for transfers between devices: 41.6 us -> 0 us
  matrix products: 24.2 us -> 0 us
  starting transfers between devices: 17.2 us -> 0 us
  between operations: 14.1 us -> 0.66 us
  local copies, waits for them, and re-layouts: 4.82 us -> 9.7 us
  other arithmetic: 4.45 us -> 0 us
    pallas_call x0 -> x1, Pallas kernels: none -> 45.7 us  [shards(): pl.pallas_call(functools.partial(kernel, sections, experts, replicas, cap...]
    all_to_all x4 -> x0, waiting for transfers between devices: 30 us -> none  [the longest x1 8.99 us: shards(): lax.all_to_all(backward_buffer, 'expert', split_axis=0, concat_axis=0, ti...]
    dot_general x12 -> x0, matrix products: 24.2 us -> none  [the longest x2 4.82 us: pack_rows(): lax.dot_general(table, values, (((0,), (0,)), ((), ())), preferred_elemen...]
    all_to_all x4 -> x0, starting transfers between devices: 17.2 us -> none  [the longest x1 5.16 us: shards(): lax.all_to_all(backward_buffer, 'expert', split_axis=0, concat_axis=0, ti...]
    reduce_scatter x1 -> x0, waiting for transfers between devices: 11.6 us -> none  [shards(): lax.psum_scatter(lax.dot_general(saved, both_grads, (((0,), (0,)), ((), (...]
    unnamed x16 -> x19, local copies, waits for them, and re-layouts: 4.82 us -> 9.7 us
    convert_element_type x2 -> x0, other arithmetic: 1.6 us -> none  [route_table(): (flat_ids[:, None] == jnp.arange(experts, dtype=jnp.int32)[None, :]).asty...]
    another operation x2 -> x0, other arithmetic: 1.18 us -> none  [route_table(): earlier = jnp.cumsum(member, axis=0) - member]
  transfers between devices with their start and end apart: 6 -> 0, of which waited for: 5 -> 0; matrix products, arithmetic and copies ran while one was open for 17% -> 0% of each run, Pallas kernels for 0% -> 0%
where the time goes in v1:
time: 56.3 us; the launch traced here: 56 us
  Pallas kernels  45.7 us (81%)
  local copies, waits for them, and re-layouts  9.7 us (17%)
  between operations  0.66 us (1%)
    pallas_call x1, Pallas kernels, shards(): pl.pallas_call(functools.partial(kernel, sections, experts, replicas, cap...  45.7 us
    unnamed x19, local copies, waits for them, and re-layouts  9.7 us

profile of v1, /device:TPU:0, one launch (start us, length us, event | category | flops | bytes accessed | tf_op | source)
XLA Modules:
  0.0 56.0 jit_solution(4848480590256604594)
XLA Ops:
  0.6 0.0 copy-start
  0.6 1.4 %copy-done = bf16[1,1,2048,384]{3,2,1,0:T(8,128)(2,1)S(1)} copy-done((bf16[1,1,2048,384]{3,2,1,0:T(8,128)(2,1)S(1)}, bf16[1,1,2048,384]{3,2,1,0:T(8,128)(2,1)}, u32[]{:S(2)}) %copy-start) | copy-done | bytes 1572888
  2.0 0.0 copy-start.1
  2.0 1.1 %copy-done.1 = bf16[1,1,192,2048]{3,2,1,0:T(8,128)(2,1)S(1)} copy-done((bf16[1,1,192,2048]{3,2,1,0:T(8,128)(2,1)S(1)}, bf16[1,1,192,2048]{3,2,1,0:T(8,128)(2,1)}, u32[]{:S(2)}) %copy-start.1) | copy-done | bytes 786456
  3.2 0.0 copy-start.2
  3.2 1.0 %copy-done.2 = bf16[1,128,2048]{2,1,0:T(8,128)(2,1)S(1)} copy-done((bf16[1,128,2048]{2,1,0:T(8,128)(2,1)S(1)}, bf16[1,128,2048]{2,1,0:T(8,128)(2,1)}, u32[]{:S(2)}) %copy-start.2) | copy-done | bytes 524312
  4.2 0.0 copy-start.3
  4.2 1.0 %copy-done.3 = bf16[1,128,2048]{2,1,0:T(8,128)(2,1)S(1)} copy-done((bf16[1,128,2048]{2,1,0:T(8,128)(2,1)S(1)}, bf16[1,128,2048]{2,1,0:T(8,128)(2,1)}, u32[]{:S(2)}) %copy-start.3) | copy-done | bytes 524312
  5.3 0.0 copy-start.4
  5.3 0.7 %copy-done.4 = s32[1,128,1]{1,2,0:T(1,128)S(1)} copy-done((s32[1,128,1]{1,2,0:T(1,128)S(1)}, s32[1,128,1]{1,2,0:T(1,128)}, u32[]{:S(2)}) %copy-start.4) | copy-done | bytes 536
  5.9 0.0 copy-start.5
  5.9 0.7 %copy-done.5 = f32[1,128,1]{1,2,0:T(1,128)S(1)} copy-done((f32[1,128,1]{1,2,0:T(1,128)S(1)}, f32[1,128,1]{1,2,0:T(1,128)}, u32[]{:S(2)}) %copy-start.5) | copy-done | bytes 536
  6.6 0.0 copy-start.6
  6.6 0.7 %copy-done.6 = s32[1,128,1]{1,2,0:T(1,128)S(1)} copy-done((s32[1,128,1]{1,2,0:T(1,128)S(1)}, s32[1,128,1]{1,2,0:T(1,128)}, u32[]{:S(2)}) %copy-start.6) | copy-done | bytes 536
  7.2 0.0 copy-start.7
  7.2 0.7 %copy-done.7 = f32[1,128,1]{1,2,0:T(1,128)S(1)} copy-done((f32[1,128,1]{1,2,0:T(1,128)S(1)}, f32[1,128,1]{1,2,0:T(1,128)}, u32[]{:S(2)}) %copy-start.7) | copy-done | bytes 536
  7.9 45.7 %shard_map.121 = (bf16[128,2048]{1,0:T(8,128)(2,1)S(1)}, bf16[128,2048]{1,0:T(8,128)(2,1)S(1)}, bf16[512,768]{1,0:T(8,128)(2,1)S(1)}) custom-call(s32[1,128]{1,0:T(1,128)S(1)} %bitcast.20, f32[1,128]{1,0:T(1,128)S(1)} %bitcast.21, s32[1,128]{1,0:T(1,128)S(1)} %bitcast.22, f32[1,128]{1,0:T(1,128)S(1)} %bitcast.23, bf16[128,2048]{1,0:T(8,128)(2,1)S(1)} %bitcast.16, ...), custom_call_target="tpu_custom_call" | custom-call | tf_op jit(solution)/shard_map/pallas_call | solution.py:289
  53.5 0.8 %copy.16 = bf16[1,128,2048]{2,1,0:T(8,128)(2,1)} copy(bf16[1,128,2048]{2,1,0:T(8,128)(2,1)S(1)} %bitcast.19) | data formatting | bytes 1048576
  54.3 0.8 %copy.17 = bf16[1,128,2048]{2,1,0:T(8,128)(2,1)} copy(bf16[1,128,2048]{2,1,0:T(8,128)(2,1)S(1)} %bitcast.18) | data formatting | bytes 1048576
  55.1 0.9 %copy.18 = bf16[1,1,512,768]{3,2,1,0:T(8,128)(2,1)} copy(bf16[1,1,512,768]{3,2,1,0:T(8,128)(2,1)S(1)} %bitcast.15) | data formatting | bytes 1572864
Async XLA Ops:
  0.6 1.4 %copy-start = (bf16[1,1,2048,384]{3,2,1,0:T(8,128)(2,1)S(1)}, bf16[1,1,2048,384]{3,2,1,0:T(8,128)(2,1)}, u32[]{:S(2)}) copy-start(bf16[1,1,2048,384]{3,2,1,0:T(8,128)(2,1)} %param.17) | copy-start | bytes 4718596
  2.0 1.1 %copy-start.1 = (bf16[1,1,192,2048]{3,2,1,0:T(8,128)(2,1)S(1)}, bf16[1,1,192,2048]{3,2,1,0:T(8,128)(2,1)}, u32[]{:S(2)}) copy-start(bf16[1,1,192,2048]{3,2,1,0:T(8,128)(2,1)} %param.16) | copy-start | bytes 2359300
  3.2 1.0 %copy-start.2 = (bf16[1,128,2048]{2,1,0:T(8,128)(2,1)S(1)}, bf16[1,128,2048]{2,1,0:T(8,128)(2,1)}, u32[]{:S(2)}) copy-start(bf16[1,128,2048]{2,1,0:T(8,128)(2,1)} %param.10) | copy-start | bytes 1572868
  4.2 1.0 %copy-start.3 = (bf16[1,128,2048]{2,1,0:T(8,128)(2,1)S(1)}, bf16[1,128,2048]{2,1,0:T(8,128)(2,1)}, u32[]{:S(2)}) copy-start(bf16[1,128,2048]{2,1,0:T(8,128)(2,1)} %param.13) | copy-start | bytes 1572868
  5.3 0.7 %copy-start.4 = (s32[1,128,1]{1,2,0:T(1,128)S(1)}, s32[1,128,1]{1,2,0:T(1,128)}, u32[]{:S(2)}) copy-start(s32[1,128,1]{1,2,0:T(1,128)} %param.11) | copy-start | bytes 1540
  5.9 0.7 %copy-start.5 = (f32[1,128,1]{1,2,0:T(1,128)S(1)}, f32[1,128,1]{1,2,0:T(1,128)}, u32[]{:S(2)}) copy-start(f32[1,128,1]{1,2,0:T(1,128)} %param.12) | copy-start | bytes 1540
  6.6 0.7 %copy-start.6 = (s32[1,128,1]{1,2,0:T(1,128)S(1)}, s32[1,128,1]{1,2,0:T(1,128)}, u32[]{:S(2)}) copy-start(s32[1,128,1]{1,2,0:T(1,128)} %param.14) | copy-start | bytes 1540
  7.2 0.7 %copy-start.7 = (f32[1,128,1]{1,2,0:T(1,128)S(1)}, f32[1,128,1]{1,2,0:T(1,128)}, u32[]{:S(2)}) copy-start(f32[1,128,1]{1,2,0:T(1,128)} %param.15) | copy-start | bytes 1540

commit v2 on v1

--- a/solution.py
+++ b/solution.py
@@ -9,6 +9,7 @@
 
 MESH = pl.DeviceIdType.MESH
 BF16, F32 = jnp.bfloat16, jnp.float32
+PARTS = 2
 
 
 def flipped(index, mask):
@@ -52,7 +53,7 @@
     f_routes, f_gates, b_routes, b_gates, tokens_hbm, cot_hbm, saved_hbm, gate_hbm, up_hbm, down_hbm,
     out_hbm, received_hbm, grads_hbm,
     tokens, cot, saved, w_gu, w_down, f_send, f_recv, b_send, b_recv,
-    o_send, o_recv, r_send, r_recv, x_all, g_all, pre, out_v, local_v, grads_v,
+    o_send, o_recv, r_send, r_recv, x_all, g_all, pre, out_v, local_v, grads_v, total,
     local_sem, a2a_send, a2a_recv, x_send, x_recv, g_send, g_recv, s_send, s_recv, out_sem,
 ):
     section, me, rep = lax.axis_index("section"), lax.axis_index("expert"), lax.axis_index("replica")
@@ -112,25 +113,28 @@
     b_scale = to_column(b_gates[...])
     loads[0].wait()
     scaled = (b_scale * cot[...].astype(F32)).astype(BF16)
-    phases = [[], [], [], []]
-    for k in order:
+    phases = [
+        [exchange(phase, k, src, dst) for k in order]
+        for phase, (src, dst) in enumerate(
+            [(b_send, b_recv), (f_send, f_recv), (r_send, r_recv), (o_send, o_recv)]
+        )
+    ]
+    x_copies = [
+        pltpu.make_async_remote_copy(
+            src_ref=saved_hbm.at[:, pl.ds(pl.multiple_of((rep + k) % replicas * share, share), share)],
+            dst_ref=x_all.at[pl.ds(pl.multiple_of(rep * rows, rows), rows)],
+            send_sem=x_send.at[k], recv_sem=x_recv.at[k],
+            device_id={"replica": (rep + k) % replicas}, device_id_type=MESH,
+        )
+        for k in range(1, replicas)
+    ]
+    for k, copy in zip(order, phases[0]):
         block(b_send, flipped(me, k))[...] = pack(b_row, scaled, flipped(me, k))
         if k == order[0]:
             pl.semaphore_wait(barrier, greeted)
-        copy = exchange(0, k, b_send, b_recv)
         copy.start()
-        phases[0].append(copy)
-    x_copies = []
-    for k in range(1, replicas):
-        other = (rep + k) % replicas
-        copy = pltpu.make_async_remote_copy(
-            src_ref=saved_hbm.at[:, pl.ds(pl.multiple_of(other * share, share), share)],
-            dst_ref=x_all.at[pl.ds(pl.multiple_of(rep * rows, rows), rows)],
-            send_sem=x_send.at[k], recv_sem=x_recv.at[k],
-            device_id={"replica": other}, device_id_type=MESH,
-        )
+    for copy in x_copies:
         copy.start()
-        x_copies.append(copy)
     block(b_recv, me)[...] = pack(b_row, scaled, me)
 
     f_row, f_column = route_slots(f_routes[...], experts, cap)
@@ -138,9 +142,6 @@
     loads[1].wait()
     for k in order:
         block(f_send, flipped(me, k))[...] = pack(f_row, tokens[...], flipped(me, k))
-        copy = exchange(1, k, f_send, f_recv)
-        copy.start()
-        phases[1].append(copy)
     block(f_recv, me)[...] = pack(f_row, tokens[...], me)
 
     loads[2].wait()
@@ -148,6 +149,15 @@
     loads[4].wait()
     pre[...] = jnp.dot(saved[...], w_gu[...], preferred_element_type=F32)
     loads[5].wait()
+    loads[6].wait()
+
+    def follow(phase):
+        for copy in phases[phase - 1]:
+            copy.wait_send()
+        for copy in phases[phase]:
+            copy.start()
+
+    follow(1)
 
     for copy in phases[0]:
         copy.wait_recv()
@@ -159,32 +169,69 @@
     g_all[mine, :hidden_units] = (
         hidden_grad * up_pre * sigma * (1.0 + gate_pre * (1.0 - sigma))
     ).astype(BF16)
-
-    def pass_on(source, side):
-        where = pl.ds(pl.multiple_of(source * rows, rows), rows)
-        other = rep + (1 if side == 0 else -1)
+    part = rows // PARTS
+
+    def pass_on(source, side, piece):
+        where = pl.ds(pl.multiple_of(source * rows + piece * part, part), part)
         return pltpu.make_async_remote_copy(
             src_ref=g_all.at[where], dst_ref=g_all.at[where],
-            send_sem=g_send.at[side, source], recv_sem=g_recv.at[source],
-            device_id={"replica": other}, device_id_type=MESH,
-        )
-
-    @pl.when(rep < replicas - 1)
-    def _():
-        pass_on(rep, 0).start()
-
-    @pl.when(rep > 0)
-    def _():
-        pass_on(rep, 1).start()
+            send_sem=g_send.at[side, source, piece], recv_sem=g_recv.at[source, piece],
+            device_id={"replica": rep + (1 if side == 0 else -1)}, device_id_type=MESH,
+        )
+
+    for piece in range(PARTS):
+        @pl.when(rep < replicas - 1)
+        def _():
+            pass_on(rep, 0, piece).start()
+
+        @pl.when(rep > 0)
+        def _():
+            pass_on(rep, 1, piece).start()
+
+    def relay(step, piece):
+        low, high = rep - step, rep + step
+
+        @pl.when(low >= 0)
+        def _():
+            pass_on(low, 0, piece).wait_recv()
+
+            @pl.when(rep < replicas - 1)
+            def _():
+                pass_on(low, 0, piece).start()
+
+        @pl.when(high < replicas)
+        def _():
+            pass_on(high, 1, piece).wait_recv()
+
+            @pl.when(rep > 0)
+            def _():
+                pass_on(high, 1, piece).start()
+
+    def term(source):
+        where = pl.ds(pl.multiple_of(source * rows, rows), rows)
+        return lax.dot_general(
+            x_all[where, :], g_all[where, :], (((0,), (0,)), ((), ())), preferred_element_type=F32
+        )
+
+    def add_terms(step):
+        low, high = rep - step, rep + step
+
+        @pl.when(low >= 0)
+        def _():
+            x_copies[step - 1].wait_recv()
+            total[...] += term(low)
+
+        @pl.when(high < replicas)
+        def _():
+            x_copies[replicas - step - 1].wait_recv()
+            total[...] += term(high)
 
     for c in range(0, width, chunk):
         r_send[:, c:c + chunk] = transposed_dot(g_all[mine, :], w_gu[c:c + chunk, :]).astype(BF16)
-    for k in order:
-        copy = exchange(2, k, r_send, r_recv)
-        copy.start()
-        phases[2].append(copy)
     block(r_recv, me)[...] = block(r_send, me)[...]
-
+    total[...] = term(rep)
+
+    follow(2)
     for copy in phases[1]:
         copy.wait_recv()
     pre[...] = jnp.dot(f_recv[...], w_gu[...], preferred_element_type=F32)
@@ -192,32 +239,12 @@
     hidden = (gate_pre * jax.nn.sigmoid(gate_pre) * up_pre).astype(BF16)
     for c in range(0, width, chunk):
         o_send[:, c:c + chunk] = transposed_dot(hidden, w_down[c:c + chunk, :]).astype(BF16)
-    for k in order:
-        copy = exchange(3, k, o_send, o_recv)
-        copy.start()
-        phases[3].append(copy)
     block(o_recv, me)[...] = block(o_send, me)[...]
 
-    def relay(step):
-        low, high = rep - step, rep + step
-
-        @pl.when(low >= 0)
-        def _():
-            pass_on(low, 0).wait_recv()
-
-            @pl.when(rep < replicas - 1)
-            def _():
-                pass_on(low, 0).start()
-
-        @pl.when(high < replicas)
-        def _():
-            pass_on(high, 1).wait_recv()
-
-            @pl.when(rep > 0)
-            def _():
-                pass_on(high, 1).start()
-
-    relay(1)
+    for piece in range(PARTS):
+        relay(1, piece)
+    follow(3)
+    add_terms(1)
 
     for copy in phases[2]:
         copy.wait_recv()
@@ -230,13 +257,10 @@
     onward.start()
 
     for step in range(2, replicas):
-        relay(step)
-    for copy in x_copies:
-        copy.wait_recv()
-    loads[6].wait()
-    grads_v[...] = lax.dot_general(
-        x_all[...], g_all[...], (((0,), (0,)), ((), ())), preferred_element_type=F32
-    ).astype(BF16)
+        for piece in range(PARTS):
+            relay(step, piece)
+        add_terms(step)
+    grads_v[...] = total[...].astype(BF16)
     store_grads = pltpu.make_async_copy(grads_v, grads_hbm, out_sem.at[0])
     store_grads.start()
 
@@ -247,19 +271,18 @@
     store_out = pltpu.make_async_copy(out_v, out_hbm, out_sem.at[1])
     store_out.start()
 
-    for phase in phases:
-        for copy in phase:
-            copy.wait_send()
-    for copy in x_copies:
+    for copy in phases[3] + x_copies:
         copy.wait_send()
     for source in range(replicas):
         @pl.when((rep >= source) & (rep < replicas - 1))
         def _():
-            pass_on(source, 0).wait_send()
+            for piece in range(PARTS):
+                pass_on(source, 0, piece).wait_send()
 
         @pl.when((rep <= source) & (rep > 0))
         def _():
-            pass_on(source, 1).wait_send()
+            for piece in range(PARTS):
+                pass_on(source, 1, piece).wait_send()
     onward.wait()
     store_grads.wait()
     store_out.wait()
@@ -309,19 +332,20 @@
                 pltpu.VMEM((count, width), BF16),
                 pltpu.VMEM((count, width), BF16),
                 pltpu.VMEM((share, 2 * hidden_units), BF16),
+                pltpu.VMEM((share, 2 * hidden_units), F32),
                 dma((7,)),
                 dma((4, experts)),
                 dma((4, experts)),
                 dma((replicas,)),
                 dma((replicas,)),
-                dma((2, replicas)),
-                dma((replicas,)),
+                dma((2, replicas, PARTS)),
+                dma((replicas, PARTS)),
                 dma,
                 dma,
                 dma((2,)),
             ],
             compiler_params=pltpu.CompilerParams(
-                collective_id=0, has_side_effects=True, vmem_limit_bytes=48 * 1024 * 1024
+                collective_id=0, has_side_effects=True, vmem_limit_bytes=62 * 1024 * 1024
             ),
         )(
             forward_routes.reshape(1, count), forward_gates.reshape(1, count),

time: 56.3 us -> 50.3 us (0.89)
  local copies, waits for them, and re-layouts: 9.7 us -> 4.72 us
  Pallas kernels: 45.7 us -> 44.7 us
    unnamed x19 -> x5, local copies, waits for them, and re-layouts: 9.7 us -> 4.72 us
    pallas_call x1, Pallas kernels: 45.7 us -> 44.7 us  [shards(): pl.pallas_call(functools.partial(kernel, sections, experts, replicas, cap...]
where the time goes in v2:
time: 50.3 us; the launch traced here: 50.1 us
  Pallas kernels  44.7 us (89%)
  local copies, waits for them, and re-layouts  4.72 us (9%)
  between operations  0.65 us (1%)
    pallas_call x1, Pallas kernels, shards(): pl.pallas_call(functools.partial(kernel, sections, experts, replicas, cap...  44.7 us
    unnamed x5, local copies, waits for them, and re-layouts  4.72 us

profile of v2, /device:TPU:0, one launch (start us, length us, event | category | flops | bytes accessed | tf_op | source)
XLA Modules:
  0.0 50.1 jit_solution(16156217280301477960)
XLA Ops:
  0.6 44.7 %shard_map.121 = (bf16[128,2048]{1,0:T(8,128)(2,1)}, bf16[128,2048]{1,0:T(8,128)(2,1)}, bf16[512,768]{1,0:T(8,128)(2,1)}) custom-call(s32[1,128]{1,0:T(1,128)} %bitcast.22, f32[1,128]{1,0:T(1,128)} %bitcast.23, s32[1,128]{1,0:T(1,128)} %bitcast.24, f32[1,128]{1,0:T(1,128)} %bitcast.25, bf16[128,2048]{1,0:T(8,128)(2,1)} %bitcast.18, ...), custom_call_target="tpu_custom_call" | custom-call | tf_op jit(solution)/shard_map/pallas_call | solution.py:312
  45.4 0.0 copy-start
  45.4 2.0 %copy.16 = bf16[1,128,2048]{2,1,0:T(8,128)(2,1)} copy(bf16[1,128,2048]{2,1,0:T(8,128)(2,1)} %bitcast.21) | data formatting | bytes 1048576
  47.3 1.9 %copy.17 = bf16[1,128,2048]{2,1,0:T(8,128)(2,1)} copy(bf16[1,128,2048]{2,1,0:T(8,128)(2,1)} %bitcast.20) | data formatting | bytes 1048576
  49.2 0.0 copy-done
  49.2 0.9 %copy.18 = bf16[1,1,512,768]{3,2,1,0:T(8,128)(2,1)} copy(bf16[1,1,512,768]{3,2,1,0:T(8,128)(2,1)S(1)} %bitcast.17) | data formatting | bytes 1572864
Async XLA Ops:
  45.4 3.8 %copy-start = (bf16[512,768]{1,0:T(8,128)(2,1)S(1)}, bf16[512,768]{1,0:T(8,128)(2,1)}, u32[]{:S(2)}) copy-start(bf16[512,768]{1,0:T(8,128)(2,1)} %get-tuple-element.8) | copy-start | bytes 2359300

commit v3 on v2

--- a/solution.py
+++ b/solution.py
@@ -50,11 +50,11 @@
 
 def kernel(
     sections, experts, replicas, cap,
-    f_routes, f_gates, b_routes, b_gates, tokens_hbm, cot_hbm, saved_hbm, gate_hbm, up_hbm, down_hbm,
-    out_hbm, received_hbm, grads_hbm,
-    tokens, cot, saved, w_gu, w_down, f_send, f_recv, b_send, b_recv,
-    o_send, o_recv, r_send, r_recv, x_all, g_all, pre, out_v, local_v, grads_v, total,
-    local_sem, a2a_send, a2a_recv, x_send, x_recv, g_send, g_recv, s_send, s_recv, out_sem,
+    f_routes_hbm, f_gates_hbm, b_routes_hbm, b_gates_hbm, tokens_hbm, cot_hbm, saved_hbm, gate_hbm, up_hbm, down_hbm,
+    out_v, received, grads_v,
+    f_routes, f_gates, b_routes, b_gates, tokens, cot, saved, w_gu, w_down, f_send, f_recv, b_send, b_recv,
+    o_send, o_recv, r_send, r_recv, x_all, g_all, pre, local_v, total,
+    local_sem, a2a_send, a2a_recv, x_send, x_recv, g_send, g_recv, s_send, s_recv,
 ):
     section, me, rep = lax.axis_index("section"), lax.axis_index("expert"), lax.axis_index("replica")
     count, width = tokens.shape
@@ -86,9 +86,13 @@
             (down_hbm, w_down),
             (saved_hbm.at[:, pl.ds(pl.multiple_of(rep * share, share), share)],
              x_all.at[pl.ds(pl.multiple_of(rep * rows, rows), rows)]),
+            (b_routes_hbm, b_routes),
+            (b_gates_hbm, b_gates),
+            (f_routes_hbm, f_routes),
+            (f_gates_hbm, f_gates),
         ])
     ]
-    for load in loads:
+    for load in loads[7:] + loads[:7]:
         load.start()
 
     def block(ref, index):
@@ -109,6 +113,8 @@
         table = (down == row).astype(F32).astype(BF16)
         return jnp.dot(table, values, preferred_element_type=F32).astype(BF16)
 
+    loads[7].wait()
+    loads[8].wait()
     b_row, b_column = route_slots(b_routes[...], experts, cap)
     b_scale = to_column(b_gates[...])
     loads[0].wait()
@@ -132,11 +138,13 @@
         block(b_send, flipped(me, k))[...] = pack(b_row, scaled, flipped(me, k))
         if k == order[0]:
             pl.semaphore_wait(barrier, greeted)
-        copy.start()
-    for copy in x_copies:
+            for x_copy in x_copies:
+                x_copy.start()
         copy.start()
     block(b_recv, me)[...] = pack(b_row, scaled, me)
 
+    loads[9].wait()
+    loads[10].wait()
     f_row, f_column = route_slots(f_routes[...], experts, cap)
     f_scale = to_column(f_gates[...])
     loads[1].wait()
@@ -251,7 +259,7 @@
     back = jnp.dot(spread_table(b_column, rows), r_recv[...], preferred_element_type=F32)
     local_v[...] = (cot[...].astype(F32) + back).astype(BF16)
     onward = pltpu.make_async_remote_copy(
-        src_ref=local_v, dst_ref=received_hbm, send_sem=s_send, recv_sem=s_recv,
+        src_ref=local_v, dst_ref=received, send_sem=s_send, recv_sem=s_recv,
         device_id={"section": (section + sections - 1) % sections}, device_id_type=MESH,
     )
     onward.start()
@@ -261,15 +269,11 @@
             relay(step, piece)
         add_terms(step)
     grads_v[...] = total[...].astype(BF16)
-    store_grads = pltpu.make_async_copy(grads_v, grads_hbm, out_sem.at[0])
-    store_grads.start()
 
     for copy in phases[3]:
         copy.wait_recv()
     back = jnp.dot(spread_table(f_column, rows), o_recv[...], preferred_element_type=F32)
     out_v[...] = (tokens[...].astype(F32) + f_scale * back).astype(BF16)
-    store_out = pltpu.make_async_copy(out_v, out_hbm, out_sem.at[1])
-    store_out.start()
 
     for copy in phases[3] + x_copies:
         copy.wait_send()
@@ -284,8 +288,15 @@
             for piece in range(PARTS):
                 pass_on(source, 1, piece).wait_send()
     onward.wait()
-    store_grads.wait()
-    store_out.wait()
+
+
+def store(out_v, received, grads_v, out_hbm, received_hbm, grads_hbm, sem):
+    pairs = [(out_v, out_hbm), (received, received_hbm), (grads_v, grads_hbm)]
+    copies = [pltpu.make_async_copy(src, dst, sem.at[i]) for i, (src, dst) in enumerate(pairs)]
+    for copy in copies:
+        copy.start()
+    for copy in copies:
+        copy.wait()
 
 
 def solution(mesh):
@@ -308,17 +319,21 @@
         buffer = pltpu.VMEM((rows, width), BF16)
         dma = pltpu.SemaphoreType.DMA
         whole = pl.BlockSpec(memory_space=pltpu.VMEM)
-        anywhere = pl.BlockSpec(memory_space=pl.ANY)
-        out, received, grads = pl.pallas_call(
+        far = pl.BlockSpec(memory_space=pltpu.HBM)
+        held = pl.pallas_call(
             functools.partial(kernel, sections, experts, replicas, cap),
             out_shape=[
-                jax.ShapeDtypeStruct((count, width), BF16),
-                jax.ShapeDtypeStruct((count, width), BF16),
-                jax.ShapeDtypeStruct((share, 2 * hidden_units), BF16),
+                pltpu.VMEM((count, width), BF16),
+                pltpu.VMEM((count, width), BF16),
+                pltpu.VMEM((share, 2 * hidden_units), BF16),
             ],
-            in_specs=[whole] * 4 + [anywhere] * 6,
-            out_specs=[anywhere] * 3,
+            in_specs=[far] * 10,
+            out_specs=[whole] * 3,
             scratch_shapes=[
+                pltpu.VMEM((1, count), jnp.int32),
+                pltpu.VMEM((1, count), F32),
+                pltpu.VMEM((1, count), jnp.int32),
+                pltpu.VMEM((1, count), F32),
                 pltpu.VMEM((count, width), BF16),
                 pltpu.VMEM((count, width), BF16),
                 buffer,
@@ -330,10 +345,8 @@
                 pltpu.VMEM((replicas * rows, 2 * hidden_units), BF16),
                 pltpu.VMEM((rows, 2 * hidden_units), F32),
                 pltpu.VMEM((count, width), BF16),
-                pltpu.VMEM((count, width), BF16),
-                pltpu.VMEM((share, 2 * hidden_units), BF16),
                 pltpu.VMEM((share, 2 * hidden_units), F32),
-                dma((7,)),
+                dma((11,)),
                 dma((4, experts)),
                 dma((4, experts)),
                 dma((replicas,)),
@@ -342,17 +355,28 @@
                 dma((replicas, PARTS)),
                 dma,
                 dma,
-                dma((2,)),
             ],
             compiler_params=pltpu.CompilerParams(
-                collective_id=0, has_side_effects=True, vmem_limit_bytes=62 * 1024 * 1024
+                collective_id=0, has_side_effects=True, vmem_limit_bytes=44 * 1024 * 1024
             ),
         )(
-            forward_routes.reshape(1, count), forward_gates.reshape(1, count),
-            backward_routes.reshape(1, count), backward_gates.reshape(1, count),
-            forward_tokens[0], backward_cotangent[0], saved,
-            gate_weight[0, 0], up_weight[0, 0], down_weight[0, 0],
-        )
+            *(
+                pltpu.with_memory_space_constraint(value, pltpu.HBM)
+                for value in (
+                    forward_routes.reshape(1, count), forward_gates.reshape(1, count),
+                    backward_routes.reshape(1, count), backward_gates.reshape(1, count),
+                    forward_tokens[0], backward_cotangent[0], saved,
+                    gate_weight[0, 0], up_weight[0, 0], down_weight[0, 0],
+                )
+            ),
+        )
+        out, received, grads = pl.pallas_call(
+            store,
+            out_shape=[jax.ShapeDtypeStruct(value.shape, value.dtype) for value in held],
+            in_specs=[whole] * 3,
+            out_specs=[far] * 3,
+            scratch_shapes=[dma((3,))],
+        )(*(pltpu.with_memory_space_constraint(value, pltpu.VMEM) for value in held))
         return out[None], received[None], grads[None, None]
 
     tokens = P("section", ("expert", "replica"), None)

time: 50.3 us -> 45.1 us (0.90)
  local copies, waits for them, and re-layouts: 4.72 us -> 0 us
    unnamed x5 -> x0, local copies, waits for them, and re-layouts: 4.72 us -> none
    pallas_call x1, Pallas kernels: 44.7 us -> 43.1 us  [shards(): pl.pallas_call(functools.partial(kernel, sections, experts, replicas, cap...]
    pallas_call x0 -> x1, Pallas kernels: none -> 1.25 us  [shards(): pl.pallas_call(store, out_shape=[jax.ShapeDtypeStruct(value.shape, value....]
where the time goes in v3:
time: 45.1 us; the launch traced here: 45 us
  Pallas kernels  44.3 us (98%)
  between operations  0.64 us (1%)
    pallas_call x1, Pallas kernels, shards(): pl.pallas_call(functools.partial(kernel, sections, experts, replicas, cap...  43.1 us
    pallas_call x1, Pallas kernels, shards(): pl.pallas_call(store, out_shape=[jax.ShapeDtypeStruct(value.shape, value....  1.25 us

profile of v3, /device:TPU:0, one launch (start us, length us, event | category | flops | bytes accessed | tf_op | source)
XLA Modules:
  0.0 45.0 jit_solution(5146354458306189990)
XLA Ops:
  0.6 43.1 %shard_map.121 = (bf16[128,2048]{1,0:T(8,128)(2,1)S(1)}, bf16[128,2048]{1,0:T(8,128)(2,1)S(1)}, bf16[512,768]{1,0:T(8,128)(2,1)S(1)}) custom-call(s32[1,128]{1,0:T(1,128)} %bitcast.19, f32[1,128]{1,0:T(1,128)} %bitcast.20, s32[1,128]{1,0:T(1,128)} %bitcast.21, f32[1,128]{1,0:T(1,128)} %bitcast.22, bf16[128,2048]{1,0:T(8,128)(2,1)} %bitcast.17, ...), custom_call_target="tpu_custom_call" | custom-call | tf_op jit(solution)/shard_map/pallas_call | solution.py:323
  43.7 1.3 %shard_map.122 = (bf16[128,2048]{1,0:T(8,128)(2,1)}, bf16[128,2048]{1,0:T(8,128)(2,1)}, bf16[512,768]{1,0:T(8,128)(2,1)}) custom-call(bf16[128,2048]{1,0:T(8,128)(2,1)S(1)} %get-tuple-element.9.out_v, bf16[128,2048]{1,0:T(8,128)(2,1)S(1)} %get-tuple-element.10.received, bf16[512,768]{1,0:T(8,128)(2,1)S(1)} %get-tuple-element.11.grads_v), custom_call_target="tpu_custom_call" | custom-call | tf_op jit(solution)/shard_map/pallas_call | solution.py:373
